TPU v7x, 32 devices: a whole 2x2x4 slice. The times are simulated.
32 devices in a mesh: pole: 4 (over y, x), row: 2 (over core), col: 4 (over z).
Axes of the slice: x: 2, y: 2, z: 4, core: 2. Of those that a mesh axis runs over, the one named last changes fastest.
Arguments:
- hamiltonian_panel: bfloat16 [6144, 512], P(('row', 'col'), 'pole'), may hold values from -0.005859375 to 0.005859375
- margin_panel: bfloat16 [6144, 512], P(('row', 'col'), 'pole'), may hold values from -0.0029296875 to 0.0029296875
- shifts: float32 [4, 2], P('pole'), may hold values from -2 to 2
- weights: float32 [4, 2], P('pole'), may hold values from 0.5 to 2
- pivot_inverse: float32 [4, 2, 512, 512], P('pole'), may hold values from -6 to 6
- selected_inverse: bfloat16 [4, 2, 6144, 6144], P('pole', None, 'row', 'col'), may hold values from -6 to 6
Outputs:
- inverse_column: float32 [4, 6144, 2, 512], P('pole', ('row', 'col'))
- inverse_pivot: float32 [4, 2, 512, 512], P('pole')
- density_column: float32 [6144, 512], P(('row', 'col'), 'pole')
- density_pivot: float32 [512, 512], P('pole')
All inputs are finite; a program needn't handle non-finite values.
Results may differ from a plain program's by a relative error of at most 0.0037.
Values may be sent and summed in bfloat16 or wider, within the bound.
A program may use at most 128 MiB of HBM per device.

v0:
```python
import jax
import jax.numpy as jnp
from jax import lax
from jax.sharding import PartitionSpec as P

HALVES = 2


def precise(left, right):
    return jnp.dot(left, right, precision=lax.Precision.HIGH, preferred_element_type=jnp.float32)


def gather_panel(pair):
    return lax.all_gather(pair, "pole", axis=2, tiled=True)


def factor_panel(pair, shift, inverse):
    hamiltonian_f = pair[0].astype(jnp.float32)
    margin_f = pair[1].astype(jnp.float32)
    real_part = hamiltonian_f - shift[0] * margin_f
    imag_part = -shift[1] * margin_f
    lower_real = precise(real_part, inverse[0]) - precise(imag_part, inverse[1])
    lower_imag = precise(real_part, inverse[1]) + precise(imag_part, inverse[0])
    return (lower_real.astype(jnp.bfloat16), lower_imag.astype(jnp.bfloat16))


def half_dot(left, right):
    return lax.dot_general(
        left, right, (((0,), (0,)), ((), ())), preferred_element_type=jnp.float32
    )


def body(hamiltonian_panel, margin_panel, shifts, weights, pivot_inverse, selected_inverse):
    shift = shifts[0]
    weight = weights[0]
    inverse = pivot_inverse[0]
    block_real = selected_inverse[0, 0]
    block_imag = selected_inverse[0, 1]
    n_row = lax.axis_size("row")
    n_col = lax.axis_size("col")
    n_pole = lax.axis_size("pole")
    width = inverse.shape[-1]
    part = width // HALVES
    own_pair = jnp.stack([hamiltonian_panel, margin_panel])
    order = [(n_row * c + r, r * n_col + c) for r in range(n_row) for c in range(n_col)]
    met_pair = gather_panel(lax.ppermute(own_pair, ("row", "col"), order))
    met_real, met_imag = factor_panel(met_pair, shift, inverse)
    partials = []
    for h in range(HALVES):
        cut = slice(h * part, (h + 1) * part)
        mine = jnp.concatenate([met_real[:, cut], met_imag[:, cut]], axis=1)
        rows = lax.all_gather(mine, "row", axis=0, tiled=True)
        turned = jnp.concatenate([rows[:, part:], -rows[:, :part]], axis=1)
        total = jnp.dot(block_imag, turned, preferred_element_type=jnp.float32) - jnp.dot(
            block_real, rows, preferred_element_type=jnp.float32
        )
        partials.append(total.astype(jnp.bfloat16))
    own_pair, partials[-1] = lax.optimization_barrier((own_pair, partials[-1]))
    own_real, own_imag = factor_panel(gather_panel(own_pair), shift, inverse)
    lower = jnp.concatenate([own_real, own_imag], axis=1)
    columns = []
    updates = []
    for h in range(HALVES):
        column = lax.psum_scatter(partials[h], "col", scatter_dimension=0, tiled=True).astype(
            jnp.float32
        )
        high = column.astype(jnp.bfloat16)
        low = (column - high.astype(jnp.float32)).astype(jnp.bfloat16)
        square = half_dot(lower, high) + half_dot(lower, low)
        update = jnp.stack(
            [
                square[:width, :part] - square[width:, part:],
                square[:width, part:] + square[width:, :part],
            ]
        )
        updates.append(lax.psum(update, ("row", "col")))
        columns.append(column.reshape(column.shape[0], 2, part))
    column = jnp.concatenate(columns, axis=2)
    pivot = inverse - jnp.concatenate(updates, axis=2)
    column_density = weight[0] * column[:, 0] - weight[1] * column[:, 1]
    share = width // n_pole
    pieces = column_density.reshape(-1, n_pole, share).swapaxes(0, 1).astype(jnp.bfloat16)
    column_share = jnp.sum(
        lax.all_to_all(pieces, "pole", 0, 0, tiled=True).astype(jnp.float32), axis=0
    )
    pivot_density = weight[0] * pivot[0] - weight[1] * pivot[1]
    pieces = pivot_density.reshape(n_pole, share, width).astype(jnp.bfloat16)
    pivot_share = jnp.sum(
        lax.all_to_all(pieces, "pole", 0, 0, tiled=True).astype(jnp.float32), axis=0
    )
    return (column[None], pivot[None], column_share, pivot_share)


def solution(mesh):
    return jax.shard_map(
        body,
        mesh=mesh,
        in_specs=(
            P(("row", "col"), "pole"),
            P(("row", "col"), "pole"),
            P("pole", None),
            P("pole", None),
            P("pole", None, None, None),
            P("pole", None, "row", "col"),
        ),
        out_specs=(
            P("pole", ("row", "col"), None, None),
            P("pole", None, None, None),
            P(("row", "col"), "pole"),
            P("pole", None),
        ),
        check_vma=False,
    )
```

profile of v0, /device:TPU:0, one launch (start us, length us, event | category | flops | bytes accessed | tf_op | source)
XLA Modules:
  0.0 350.2 jit_solution(6100513097827890616)
XLA Ops:
  11.8 42.8 %all-gather.5.cloned.1.call-done = bf16[2,768,512]{2,1,0:T(8,128)(2,1)} async-done(((bf16[2,768,128]{2,1,0:T(8,128)(2,1)}), bf16[2,768,512]{2,1,0:T(8,128)(2,1)}) %all-gather.5.cloned.1.call-update) | async-done | bytes 1572880 | tf_op jit(solution)/shard_map/all_gather | solution.py:14
  54.6 3.2 fusion.28
  57.9 2.9 fusion.26
  60.7 2.3 subtract_convert_fusion.5
  63.0 2.3 add_convert_fusion.1
  67.5 8.9 %all-gather.9.cloned.1.call-done = bf16[1536,512]{0,1:T(8,128)(2,1)} async-done(((bf16[768,512]{0,1:T(8,128)(2,1)}), bf16[1536,512]{0,1:T(8,128)(2,1)}) %all-gather.9.cloned.1.call-update) | async-done | bytes 1572880 | tf_op jit(solution)/shard_map/all_gather | solution.py:52
  76.3 9.2 %fusion = f32[512,3072]{1,0:T(8,128)S(1)} fusion(bf16[1536,512]{0,1:T(8,128)(2,1)} %all-gather.9.cloned.1.call-done, bf16[1,2,3072,1536]{3,2,1,0:T(8,128)(2,1)} %param.11), kind=kOutput, calls=%fused_computation | convolution fusion | flops 4831838208 | bytes 17301504 | tf_op jit(solution)/shard_map/dot_general | solution.py:54
  85.7 11.0 %fusion.19 = bf16[3072,512]{0,1:T(8,128)(2,1)} fusion(f32[512,3072]{1,0:T(8,128)S(1)} %fusion, bf16[1,2,3072,1536]{3,2,1,0:T(8,128)(2,1)} %param.11, bf16[1536,256]{0,1:T(8,128)(2,1)S(1)} %get-tuple-element.25, bf16[1536,256]{0,1:T(8,128)(2,1)S(1)} %get-tuple-element.24), kind=kOutput, calls=%fused_computation.20 | convolution fusion | flops 4838129664 | bytes 20447232 | tf_op jit(solution)/shard_map/dot_general | solution.py:54
  99.4 7.7 %fusion.2 = f32[512,3072]{1,0:T(8,128)S(1)} fusion(bf16[1536,512]{0,1:T(8,128)(2,1)S(1)} %copy-done.6, bf16[1,2,3072,1536]{3,2,1,0:T(8,128)(2,1)} %param.11), kind=kOutput, calls=%fused_computation.2 | convolution fusion | flops 4831838208 | bytes 17301504 | tf_op jit(solution)/shard_map/dot_general | solution.py:54
  107.1 10.6 %fusion.16 = bf16[3072,512]{0,1:T(8,128)(2,1)} fusion(f32[512,3072]{1,0:T(8,128)S(1)} %fusion.2, bf16[1,2,3072,1536]{3,2,1,0:T(8,128)(2,1)} %param.11, bf16[1536,256]{0,1:T(8,128)(2,1)S(1)} %get-tuple-element.23, bf16[1536,256]{0,1:T(8,128)(2,1)S(1)} %get-tuple-element.22), kind=kOutput, calls=%fused_computation.19 | convolution fusion | flops 4838129664 | bytes 20447232 | tf_op jit(solution)/shard_map/dot_general | solution.py:54
  117.7 11.2 %all-gather.11.cloned.1.call-done = bf16[2,768,512]{2,1,0:T(8,128)(2,1)} async-done(((bf16[2,768,128]{2,1,0:T(8,128)(2,1)}), bf16[2,768,512]{2,1,0:T(8,128)(2,1)}) %all-gather.11.cloned.1.call-update) | async-done | bytes 1572880 | tf_op jit(solution)/shard_map/all_gather | solution.py:14
  128.9 3.7 %fusion.53 = f32[768,512]{0,1:T(8,128)S(1)} fusion(f32[1,2,512,512]{3,2,1,0:T(8,128)S(1)} %copy-done, f32[]{:T(128)} %bitcast.2, bf16[2,768,512]{2,1,0:T(8,128)(2,1)} %all-gather.11.cloned.1.call-done), kind=kOutput, calls=%fused_computation.60 | convolution fusion | flops 1209532416 | bytes 4194308 | tf_op jit(solution)/shard_map/dot_general | solution.py:10
  136.6 2.5 subtract_convert_fusion.4
  139.1 52.8 %reduce-scatter.5.cloned.1.call-done = bf16[768,512]{0,1:T(8,128)(2,1)} async-done(((bf16[3072,512]{0,1:T(8,128)(2,1)}), bf16[768,512]{0,1:T(8,128)(2,1)}) %reduce-scatter.5.cloned.1.call-update) | async-done | bytes 786448 | tf_op jit(solution)/shard_map/reduce_scatter | solution.py:64
  191.9 2.5 fusion.105
  195.6 58.8 %reduce-scatter.3.cloned.1.call-done = bf16[768,512]{0,1:T(8,128)(2,1)} async-done(((bf16[3072,512]{0,1:T(8,128)(2,1)}), bf16[768,512]{0,1:T(8,128)(2,1)}) %reduce-scatter.3.cloned.1.call-update) | async-done | bytes 786448 | tf_op jit(solution)/shard_map/reduce_scatter | solution.py:64
  254.4 2.8 fusion.106
  266.0 5.7 %copy.13 = f32[1,768,2,512]{3,2,1,0:T(2,128)} copy(f32[1,768,2,512]{1,3,2,0:T(8,128)} %fusion.22) | data formatting | bytes 6291456
  271.7 4.3 %fusion.40 = bf16[768,1,512]{0,2,1:T(8,128)(2,1)} fusion(f32[768,2,256]{0,2,1:T(8,128)} %copy-done.2, f32[768,2,256]{0,2,1:T(8,128)} %copy-done.1, f32[]{:T(128)} %bitcast.24, f32[]{:T(128)} %bitcast.23), kind=kLoop, calls=%fused_computation.43 | loop fusion | flops 2359296 | bytes 3932168 | tf_op jit(solution)/shard_map/convert_element_type | solution.py:82
  276.0 4.2 %all-to-all-start = ((bf16[4,768,128]{1,2,0:T(8,128)(2,1)}), bf16[4,768,128]{1,2,0:T(8,128)(2,1)}, u32[]{:S(2)}, u32[]{:S(2)}) async-start(bf16[4,768,128]{1,2,0:T(8,128)(2,1)} %bitcast.26), calls=%async_computation.2 | async-start | bytes 1572864 | tf_op jit(solution)/shard_map/all_to_all | solution.py:84
  280.2 45.3 %all-reduce.3.cloned.1.call-done = (f32[2,512,256]{2,1,0:T(8,128)}, f32[2,512,256]{2,1,0:T(8,128)}) async-done(((f32[2,512,256]{2,1,0:T(8,128)}, f32[2,512,256]{2,1,0:T(8,128)}), (f32[2,512,256]{2,1,0:T(8,128)}, f32[2,512,256]{2,1,0:T(8,128)})) %all-reduce.3.cloned.1.call-update) | async-done | bytes 2097168 | tf_op jit(solution)/shard_map/psum | solution.py:76
  327.5 2.4 fusion.60
  329.9 4.3 %all-to-all-start.1 = ((bf16[4,128,512]{2,1,0:T(8,128)(2,1)}), bf16[4,128,512]{2,1,0:T(8,128)(2,1)}, u32[]{:S(2)}, u32[]{:S(2)}) async-start(bf16[4,128,512]{2,1,0:T(8,128)(2,1)} %bitcast.94), calls=%async_computation.3 | async-start | bytes 1048576 | tf_op jit(solution)/shard_map/all_to_all | solution.py:89
  336.4 2.9 maximum_subtract_fusion
  (80 shorter events, 31.0 us)
Async XLA Ops:
  7.2 47.4 %all-gather.5.cloned.1.call-start = ((), (), s32[]{:S(2)}) async-start(), calls=%async_computation.4 | async-start | bytes 1966080 | tf_op jit(solution)/shard_map/all_gather | solution.py:14
  8.3 49.6 %copy-start.8 = (bf16[2,768,128]{2,1,0:T(8,128)(2,1)}, bf16[2,768,128]{2,1,0:T(8,128)(2,1)S(1)}, u32[]{:S(2)}) copy-start(bf16[2,768,128]{2,1,0:T(8,128)(2,1)S(1)} %pad_maximum_fusion.6) | copy-start | bytes 1179652
  8.3 0.7 collective-permute-start
  9.8 66.6 %all-gather.9.cloned.1.call-start = ((), (), s32[]{:S(2)}) async-start(), calls=%async_computation.7 | async-start | bytes 2359296 | tf_op jit(solution)/shard_map/all_gather | solution.py:52
  54.6 3.2 copy-start
  57.9 2.9 copy-start.4
  66.4 31.1 %all-gather.7.cloned.1.call-start = ((), (), s32[]{:S(2)}) async-start(), calls=%async_computation.5 | async-start | bytes 2359296 | tf_op jit(solution)/shard_map/all_gather | solution.py:52
  67.4 61.5 %all-gather.11.cloned.1.call-start = ((), (), s32[]{:S(2)}) async-start(), calls=%async_computation.9 | async-start | bytes 1966080 | tf_op jit(solution)/shard_map/all_gather | solution.py:14
  76.3 9.2 %copy-start.7 = (bf16[1536,512]{0,1:T(8,128)(2,1)S(1)}, bf16[1536,512]{0,1:T(8,128)(2,1)}, u32[]{:S(2)}) copy-start(bf16[1536,512]{0,1:T(8,128)(2,1)} %all-gather.9.cloned.1.call-done) | copy-start | bytes 4718596
  96.7 95.2 %reduce-scatter.5.cloned.1.call-start = ((), (), s32[]{:S(2)}) async-start(), calls=%async_computation.8 | async-start | bytes 3932160 | tf_op jit(solution)/shard_map/reduce_scatter | solution.py:64
  97.3 157.1 %reduce-scatter.3.cloned.1.call-start = ((), (), s32[]{:S(2)}) async-start(), calls=%async_computation.6 | async-start | bytes 3932160 | tf_op jit(solution)/shard_map/reduce_scatter | solution.py:64
  97.5 1.9 copy-start.6
  117.7 207.9 %all-reduce.3.cloned.1.call-start = ((), (), s32[]{:S(2)}) async-start(), calls=%async_computation.10 | async-start | bytes 4194304 | tf_op jit(solution)/shard_map/psum | solution.py:76
  128.9 3.8 %copy-start.3 = (bf16[2,768,512]{2,1,0:T(8,128)(2,1)S(1)}, bf16[2,768,512]{2,1,0:T(8,128)(2,1)}, u32[]{:S(2)}) copy-start(bf16[2,768,512]{2,1,0:T(8,128)(2,1)} %all-gather.11.cloned.1.call-done) | copy-start | bytes 4718596
  136.6 57.8 %copy-start.9 = (bf16[768,512]{0,1:T(8,128)(2,1)}, bf16[768,512]{0,1:T(8,128)(2,1)S(1)}, u32[]{:S(2)}) copy-start(bf16[768,512]{0,1:T(8,128)(2,1)S(1)} %add_convert_fusion) | copy-start | bytes 2359300
  191.9 2.5 copy-start.11
  191.9 2.5 copy-start.13
  254.4 2.8 copy-start.10
  254.4 2.8 copy-start.12
  254.4 2.8 copy-start.15
  260.5 1.2 copy-start.14
  276.0 53.9 %all-to-all-start = ((bf16[4,768,128]{1,2,0:T(8,128)(2,1)}), bf16[4,768,128]{1,2,0:T(8,128)(2,1)}, u32[]{:S(2)}, u32[]{:S(2)}) async-start(bf16[4,768,128]{1,2,0:T(8,128)(2,1)} %bitcast.26), calls=%async_computation.2 | async-start | bytes 1572864 | tf_op jit(solution)/shard_map/all_to_all | solution.py:84
  329.9 6.5 %copy-start.5 = (f32[2,512,256]{2,1,0:T(8,128)S(1)}, f32[2,512,256]{2,1,0:T(8,128)}, u32[]{:S(2)}) copy-start(f32[2,512,256]{2,1,0:T(8,128)} %get-tuple-element.16) | copy-start | bytes 3145732
  329.9 11.6 %all-to-all-start.1 = ((bf16[4,128,512]{2,1,0:T(8,128)(2,1)}), bf16[4,128,512]{2,1,0:T(8,128)(2,1)}, u32[]{:S(2)}, u32[]{:S(2)}) async-start(bf16[4,128,512]{2,1,0:T(8,128)(2,1)} %bitcast.94), calls=%async_computation.3 | async-start | bytes 1048576 | tf_op jit(solution)/shard_map/all_to_all | solution.py:89
  (5 other events, 4.9 us)
Sparse Core Ops, SparseCore 0:
  10.4 44.1 all-gather.4
  66.5 9.7 all-gather.8
  77.9 10.9 all-gather.6
  96.8 32.0 all-gather.10
  131.6 60.2 reduce-scatter.4
  194.0 60.2 reduce-scatter.2
  260.7 64.8 all-reduce.2
where the time goes:
time: 351 us; the launch traced here: 350 us
  waiting for transfers between devices  223 us (64%)
  matrix products  66.5 us (19%)
  other arithmetic  23.8 us (7%)
  between operations  15.1 us (4%)
  local copies, waits for them, and re-layouts  12.5 us (4%)
  starting transfers between devices  9.61 us (3%)
    reduce_scatter x2, waiting for transfers between devices, body(): lax.psum_scatter(partials[h], 'col', scatter_dimension=0, tiled=True)  112 us
    all_gather x2, waiting for transfers between devices, gather_panel(): return lax.all_gather(pair, 'pole', axis=2, tiled=True)  54 us
    psum x1, waiting for transfers between devices, body(): updates.append(lax.psum(update, ('row', 'col')))  45.3 us
    dot_general x2, matrix products, body(): jnp.dot(block_imag, turned, preferred_element_type=jnp.float32)  21.5 us
    dot_general x8, matrix products, precise(): jnp.dot(left, right, precision=lax.Precision.HIGH, preferred_element_type...  20.8 us
    dot_general x2, matrix products, body(): jnp.dot(block_real, rows, preferred_element_type=jnp.float32)  16.9 us
    unnamed x40, local copies, waits for them, and re-layouts  10.5 us
    all_gather x2, waiting for transfers between devices, body(): rows = lax.all_gather(mine, 'row', axis=0, tiled=True)  8.9 us
  transfers between devices with their start and end apart: 10, of which 7 were waited for; matrix products, arithmetic and copies ran while one was open for 22% of the time, Pallas kernels for 0%

commit v1 on v0

--- a/solution.py
+++ b/solution.py
@@ -73,7 +73,15 @@
                 square[:width, part:] + square[width:, :part],
             ]
         )
-        updates.append(lax.psum(update, ("row", "col")))
+
+        def compute_the_stops_all(chunk):
+            which_axis = "col"
+            chip_axis = "row"
+            for idx in (which_axis, chip_axis):
+                chunk = lax.psum(chunk, idx)
+            return chunk
+
+        updates.append(compute_the_stops_all(update))
         columns.append(column.reshape(column.shape[0], 2, part))
     column = jnp.concatenate(columns, axis=2)
     pivot = inverse - jnp.concatenate(updates, axis=2)

time: 351 us -> 399 us (1.14)
  waiting for transfers between devices: 223 us -> 272 us
    psum x1 -> x2, waiting for transfers between devices: 45.3 us -> 90.9 us  [compute_the_stops_all(): chunk = lax.psum(chunk, idx)]
  transfers between devices with their start and end apart: 10 -> 11, of which waited for: 7 -> 9; matrix products, arithmetic and copies ran while one was open for 22% -> 20% of each run, Pallas kernels for 0% -> 0%
where the time goes in v1:
time: 399 us; the launch traced here: 398 us
  waiting for transfers between devices  272 us (68%)
  matrix products  66.5 us (17%)
  other arithmetic  23.7 us (6%)
  between operations  15.2 us (4%)
  local copies, waits for them, and re-layouts  11.9 us (3%)
  starting transfers between devices  9.52 us (2%)
    reduce_scatter x2, waiting for transfers between devices, body(): lax.psum_scatter(partials[h], 'col', scatter_dimension=0, tiled=True)  112 us
    psum x2, waiting for transfers between devices, compute_the_stops_all(): chunk = lax.psum(chunk, idx)  90.9 us
    all_gather x2, waiting for transfers between devices, gather_panel(): return lax.all_gather(pair, 'pole', axis=2, tiled=True)  54 us
    dot_general x2, matrix products, body(): jnp.dot(block_imag, turned, preferred_element_type=jnp.float32)  21.5 us
    dot_general x8, matrix products, precise(): jnp.dot(left, right, precision=lax.Precision.HIGH, preferred_element_type...  20.8 us
    dot_general x2, matrix products, body(): jnp.dot(block_real, rows, preferred_element_type=jnp.float32)  16.9 us
    unnamed x40, local copies, waits for them, and re-layouts  9.91 us
    all_gather x2, waiting for transfers between devices, body(): rows = lax.all_gather(mine, 'row', axis=0, tiled=True)  8.9 us
  transfers between devices with their start and end apart: 11, of which 9 were waited for; matrix products, arithmetic and copies ran while one was open for 20% of the time, Pallas kernels for 0%

profile of v1, /device:TPU:0, one launch (start us, length us, event | category | flops | bytes accessed | tf_op | source)
XLA Modules:
  0.0 398.3 jit_solution(6540354583518662620)
XLA Ops:
  11.8 42.8 %all-gather.5.cloned.1.call-done = bf16[2,768,512]{2,1,0:T(8,128)(2,1)} async-done(((bf16[2,768,128]{2,1,0:T(8,128)(2,1)}), bf16[2,768,512]{2,1,0:T(8,128)(2,1)}) %all-gather.5.cloned.1.call-update) | async-done | bytes 1572880 | tf_op jit(solution)/shard_map/all_gather | solution.py:14
  54.6 3.2 fusion.28
  57.9 2.9 fusion.26
  67.5 8.9 %all-gather.9.cloned.1.call-done = bf16[1536,512]{0,1:T(8,128)(2,1)} async-done(((bf16[768,512]{0,1:T(8,128)(2,1)}), bf16[1536,512]{0,1:T(8,128)(2,1)}) %all-gather.9.cloned.1.call-update) | async-done | bytes 1572880 | tf_op jit(solution)/shard_map/all_gather | solution.py:52
  76.3 9.2 %fusion = f32[512,3072]{1,0:T(8,128)S(1)} fusion(bf16[1536,512]{0,1:T(8,128)(2,1)} %all-gather.9.cloned.1.call-done, bf16[1,2,3072,1536]{3,2,1,0:T(8,128)(2,1)} %param.11), kind=kOutput, calls=%fused_computation | convolution fusion | flops 4831838208 | bytes 17301504 | tf_op jit(solution)/shard_map/dot_general | solution.py:54
  85.7 11.0 %fusion.19 = bf16[3072,512]{0,1:T(8,128)(2,1)} fusion(f32[512,3072]{1,0:T(8,128)S(1)} %fusion, bf16[1,2,3072,1536]{3,2,1,0:T(8,128)(2,1)} %param.11, bf16[1536,256]{0,1:T(8,128)(2,1)S(1)} %get-tuple-element.27, bf16[1536,256]{0,1:T(8,128)(2,1)S(1)} %get-tuple-element.26), kind=kOutput, calls=%fused_computation.20 | convolution fusion | flops 4838129664 | bytes 20447232 | tf_op jit(solution)/shard_map/dot_general | solution.py:54
  99.4 7.7 %fusion.2 = f32[512,3072]{1,0:T(8,128)S(1)} fusion(bf16[1536,512]{0,1:T(8,128)(2,1)S(1)} %copy-done.6, bf16[1,2,3072,1536]{3,2,1,0:T(8,128)(2,1)} %param.11), kind=kOutput, calls=%fused_computation.2 | convolution fusion | flops 4831838208 | bytes 17301504 | tf_op jit(solution)/shard_map/dot_general | solution.py:54
  107.1 10.6 %fusion.16 = bf16[3072,512]{0,1:T(8,128)(2,1)} fusion(f32[512,3072]{1,0:T(8,128)S(1)} %fusion.2, bf16[1,2,3072,1536]{3,2,1,0:T(8,128)(2,1)} %param.11, bf16[1536,256]{0,1:T(8,128)(2,1)S(1)} %get-tuple-element.25, bf16[1536,256]{0,1:T(8,128)(2,1)S(1)} %get-tuple-element.24), kind=kOutput, calls=%fused_computation.19 | convolution fusion | flops 4838129664 | bytes 20447232 | tf_op jit(solution)/shard_map/dot_general | solution.py:54
  117.7 11.2 %all-gather.11.cloned.1.call-done = bf16[2,768,512]{2,1,0:T(8,128)(2,1)} async-done(((bf16[2,768,128]{2,1,0:T(8,128)(2,1)}), bf16[2,768,512]{2,1,0:T(8,128)(2,1)}) %all-gather.11.cloned.1.call-update) | async-done | bytes 1572880 | tf_op jit(solution)/shard_map/all_gather | solution.py:14
  128.9 3.7 fusion.53
  136.6 2.5 subtract_convert_fusion.4
  139.1 52.8 %reduce-scatter.5.cloned.1.call-done = bf16[768,512]{0,1:T(8,128)(2,1)} async-done(((bf16[3072,512]{0,1:T(8,128)(2,1)}), bf16[768,512]{0,1:T(8,128)(2,1)}) %reduce-scatter.5.cloned.1.call-update) | async-done | bytes 786448 | tf_op jit(solution)/shard_map/reduce_scatter | solution.py:64
  191.9 2.5 fusion.105
  195.6 58.8 %reduce-scatter.3.cloned.1.call-done = bf16[768,512]{0,1:T(8,128)(2,1)} async-done(((bf16[3072,512]{0,1:T(8,128)(2,1)}), bf16[768,512]{0,1:T(8,128)(2,1)}) %reduce-scatter.3.cloned.1.call-update) | async-done | bytes 786448 | tf_op jit(solution)/shard_map/reduce_scatter | solution.py:64
  254.4 2.8 fusion.106
  260.5 87.2 %all-reduce.5.cloned.1.call-done = (f32[2,512,256]{2,1,0:T(8,128)}, f32[2,512,256]{2,1,0:T(8,128)}) async-done(((f32[2,512,256]{2,1,0:T(8,128)}, f32[2,512,256]{2,1,0:T(8,128)}), (f32[2,512,256]{2,1,0:T(8,128)}, f32[2,512,256]{2,1,0:T(8,128)})) %all-reduce.5.cloned.1.call-update) | async-done | bytes 2097168 | tf_op jit(solution)/shard_map/psum | solution.py:81
  352.5 5.8 %copy.13 = f32[1,768,2,512]{3,2,1,0:T(2,128)} copy(f32[1,768,2,512]{1,3,2,0:T(8,128)} %fusion.22) | data formatting | bytes 6291456
  358.3 4.3 %fusion.40 = bf16[768,1,512]{0,2,1:T(8,128)(2,1)} fusion(f32[768,2,256]{0,2,1:T(8,128)} %copy-done.2, f32[768,2,256]{0,2,1:T(8,128)} %copy-done.1, f32[]{:T(128)} %bitcast.24, f32[]{:T(128)} %bitcast.23), kind=kLoop, calls=%fused_computation.43 | loop fusion | flops 2359296 | bytes 3932168 | tf_op jit(solution)/shard_map/convert_element_type | solution.py:90
  362.6 4.2 %all-to-all-start = ((bf16[4,768,128]{1,2,0:T(8,128)(2,1)}), bf16[4,768,128]{1,2,0:T(8,128)(2,1)}, u32[]{:S(2)}, u32[]{:S(2)}) async-start(bf16[4,768,128]{1,2,0:T(8,128)(2,1)} %bitcast.26), calls=%async_computation.2 | async-start | bytes 1572864 | tf_op jit(solution)/shard_map/all_to_all | solution.py:92
  366.8 3.7 all-reduce.7.cloned.1.call-done
  374.8 3.1 all-to-all-done
  377.9 4.1 %all-to-all-start.1 = ((bf16[4,128,512]{2,1,0:T(8,128)(2,1)}), bf16[4,128,512]{2,1,0:T(8,128)(2,1)}, u32[]{:S(2)}, u32[]{:S(2)}) async-start(bf16[4,128,512]{2,1,0:T(8,128)(2,1)} %bitcast.94), calls=%async_computation.3 | async-start | bytes 1048576 | tf_op jit(solution)/shard_map/all_to_all | solution.py:97
  384.3 2.9 maximum_subtract_fusion
  387.2 2.5 all-to-all-done.1
  (83 shorter events, 35.0 us)
Async XLA Ops:
  7.2 47.4 %all-gather.5.cloned.1.call-start = ((), (), s32[]{:S(2)}) async-start(), calls=%async_computation.4 | async-start | bytes 1966080 | tf_op jit(solution)/shard_map/all_gather | solution.py:14
  8.3 49.6 %copy-start.8 = (bf16[2,768,128]{2,1,0:T(8,128)(2,1)}, bf16[2,768,128]{2,1,0:T(8,128)(2,1)S(1)}, u32[]{:S(2)}) copy-start(bf16[2,768,128]{2,1,0:T(8,128)(2,1)S(1)} %pad_maximum_fusion.6) | copy-start | bytes 1179652
  8.3 0.7 collective-permute-start
  9.8 66.6 %all-gather.9.cloned.1.call-start = ((), (), s32[]{:S(2)}) async-start(), calls=%async_computation.7 | async-start | bytes 2359296 | tf_op jit(solution)/shard_map/all_gather | solution.py:52
  54.6 3.2 copy-start
  57.9 2.9 copy-start.4
  66.4 31.1 %all-gather.7.cloned.1.call-start = ((), (), s32[]{:S(2)}) async-start(), calls=%async_computation.5 | async-start | bytes 2359296 | tf_op jit(solution)/shard_map/all_gather | solution.py:52
  67.4 61.5 %all-gather.11.cloned.1.call-start = ((), (), s32[]{:S(2)}) async-start(), calls=%async_computation.9 | async-start | bytes 1966080 | tf_op jit(solution)/shard_map/all_gather | solution.py:14
  76.3 9.2 %copy-start.7 = (bf16[1536,512]{0,1:T(8,128)(2,1)S(1)}, bf16[1536,512]{0,1:T(8,128)(2,1)}, u32[]{:S(2)}) copy-start(bf16[1536,512]{0,1:T(8,128)(2,1)} %all-gather.9.cloned.1.call-done) | copy-start | bytes 4718596
  96.7 95.2 %reduce-scatter.5.cloned.1.call-start = ((), (), s32[]{:S(2)}) async-start(), calls=%async_computation.8 | async-start | bytes 3932160 | tf_op jit(solution)/shard_map/reduce_scatter | solution.py:64
  97.3 157.1 %reduce-scatter.3.cloned.1.call-start = ((), (), s32[]{:S(2)}) async-start(), calls=%async_computation.6 | async-start | bytes 3932160 | tf_op jit(solution)/shard_map/reduce_scatter | solution.py:64
  117.7 230.0 %all-reduce.5.cloned.1.call-start = ((), (), s32[]{:S(2)}) async-start(), calls=%async_computation.10 | async-start | bytes 4194304 | tf_op jit(solution)/shard_map/psum | solution.py:81
  128.9 3.8 copy-start.3
  136.6 57.8 %copy-start.9 = (bf16[768,512]{0,1:T(8,128)(2,1)}, bf16[768,512]{0,1:T(8,128)(2,1)S(1)}, u32[]{:S(2)}) copy-start(bf16[768,512]{0,1:T(8,128)(2,1)S(1)} %add_convert_fusion) | copy-start | bytes 2359300
  191.9 2.5 copy-start.13
  254.4 2.8 copy-start.10
  254.4 2.8 copy-start.12
  254.4 2.8 copy-start.15
  260.4 87.3 %copy-start.18 = (f32[1,2]{1,0:T(1,128)S(1)}, f32[1,2]{1,0:T(1,128)}, u32[]{:S(2)}) copy-start(f32[1,2]{1,0:T(1,128)} %param.9) | copy-start | bytes 28
  260.4 87.9 %copy-start.14 = (bf16[768,512]{0,1:T(8,128)(2,1)S(1)}, bf16[768,512]{0,1:T(8,128)(2,1)}, u32[]{:S(2)}) copy-start(bf16[768,512]{0,1:T(8,128)(2,1)} %reduce-scatter.5.cloned.1.call-done) | copy-start | bytes 2359300
  260.4 110.0 %all-reduce.7.cloned.1.call-start = ((), (), s32[]{:S(2)}) async-start(), calls=%async_computation.11 | async-start | bytes 4194304 | tf_op jit(solution)/shard_map/psum | solution.py:81
  362.6 15.3 %all-to-all-start = ((bf16[4,768,128]{1,2,0:T(8,128)(2,1)}), bf16[4,768,128]{1,2,0:T(8,128)(2,1)}, u32[]{:S(2)}, u32[]{:S(2)}) async-start(bf16[4,768,128]{1,2,0:T(8,128)(2,1)} %bitcast.26), calls=%async_computation.2 | async-start | bytes 1572864 | tf_op jit(solution)/shard_map/all_to_all | solution.py:92
  374.8 9.4 %copy-start.5 = (f32[2,512,256]{2,1,0:T(8,128)S(1)}, f32[2,512,256]{2,1,0:T(8,128)}, u32[]{:S(2)}) copy-start(f32[2,512,256]{2,1,0:T(8,128)} %get-tuple-element.18) | copy-start | bytes 3145732
  377.9 11.7 %all-to-all-start.1 = ((bf16[4,128,512]{2,1,0:T(8,128)(2,1)}), bf16[4,128,512]{2,1,0:T(8,128)(2,1)}, u32[]{:S(2)}, u32[]{:S(2)}) async-start(bf16[4,128,512]{2,1,0:T(8,128)(2,1)} %bitcast.94), calls=%async_computation.3 | async-start | bytes 1048576 | tf_op jit(solution)/shard_map/all_to_all | solution.py:97
  (6 other events, 8.6 us)
Sparse Core Ops, SparseCore 0:
  10.4 44.1 all-gather.4
  66.5 9.7 all-gather.8
  77.9 10.9 all-gather.6
  96.8 32.0 all-gather.10
  131.6 60.2 reduce-scatter.4
  194.0 60.2 reduce-scatter.2
  260.5 87.0 all-reduce.4
  350.2 20.2 all-reduce.6
